TPU v7x, 32 devices: a whole 2x2x4 slice. The times are simulated.
32 devices in a mesh: ev: 4 (over z), blk: 8 (over y, x, core).
Axes of the slice: x: 2, y: 2, z: 4, core: 2. Of those that a mesh axis runs over, the one named last changes fastest.
Arguments:
- kernel_tiles: bfloat16 [4, 8, 6, 6, 2048], P('ev', 'blk'), may hold values from -6 to 6
- region: int32 [4, 8, 6], P('ev', 'blk'), may hold values from 0 to 15, as said below
- band_width: int32 [8], replicated, may hold values from 2 to 16
Outputs:
- smoothed: float32 [3, 16, 32768], P(None, None, ('ev', 'blk'))
Inputs may be any that keep to these rules, and one draw needn't show every extreme that they name: `region`: each device's 6 entries are distinct, and no more than 2 of them lie in one lateral section (numbers s * 4 to s * 4 + 3); every device has 2 in some section.
All inputs are finite; a program needn't handle non-finite values.
Results may differ from a plain program's by a relative error of at most 0.015.
Values may be sent and summed in bfloat16 or wider, within the bound.
A program may use at most 64 MiB of HBM per device.

v0:
```python
import jax
import jax.numpy as jnp
from jax import lax
from jax.sharding import PartitionSpec as P

NT = 4
LAYERS = 8


def build_smoother(band_width, depth):
    rows = jnp.arange(depth, dtype=jnp.int32)
    layer = rows // (depth // LAYERS)
    pick = (layer[:, None] == jnp.arange(LAYERS, dtype=jnp.int32)[None, :]).astype(jnp.int32)
    half = jnp.sum(pick * band_width[None, :], axis=1)
    dist = jnp.abs(rows[:, None] - rows[None, :])
    weight = jnp.maximum(half[:, None] + 1 - dist, 0).astype(jnp.float32)
    return (weight / jnp.sum(weight, axis=1, keepdims=True)).astype(jnp.bfloat16)


def shards(kernel_tiles, region, band_width):
    tiles = kernel_tiles[0, 0]
    ids = region[0, 0]
    groups = lax.axis_size("ev")
    slabs = lax.axis_size("blk")
    count, rows, width = tiles.shape
    depth_slab = rows // 3
    flat = tiles.reshape(count, rows * width)
    targets = jnp.arange(groups * NT, dtype=jnp.int32)
    onehot = (ids[None, :] == targets[:, None]).astype(jnp.bfloat16)
    spread = jnp.dot(onehot, flat, preferred_element_type=jnp.float32).astype(jnp.bfloat16)
    summed = lax.psum_scatter(spread, "ev", scatter_dimension=0, tiled=True).astype(jnp.float32)
    slab = summed.reshape(NT, 3, depth_slab, width).transpose(1, 2, 0, 3)
    slab = slab.reshape(3, depth_slab, slabs, NT * width // slabs).astype(jnp.bfloat16)
    smoother = build_smoother(band_width, depth_slab * slabs)
    return jnp.einsum(
        "ij,cjm->cim",
        smoother,
        lax.all_to_all(slab, "blk", split_axis=2, concat_axis=1, tiled=True)[:, :, 0, :],
        preferred_element_type=jnp.float32,
    )


def solution(mesh):
    in_specs = (P("ev", "blk", None, None, None), P("ev", "blk", None), P())
    out_specs = P(None, None, ("ev", "blk"))
    return jax.shard_map(shards, mesh=mesh, in_specs=in_specs, out_specs=out_specs, check_vma=False)
```

profile of v0, /device:TPU:0, one launch (start us, length us, event | category | flops | bytes accessed | tf_op | source)
XLA Modules:
  0.0 67.8 jit_solution(4100207346096389748)
XLA Ops:
  6.5 0.0 all-reduce.3.cloned.1.call-start
  6.5 1.0 %copy.12 = bf16[1,6,6,2048]{3,1,2,0:T(8,128)(2,1)S(1)} copy(bf16[1,6,6,2048]{3,2,1,0:T(8,128)(2,1)} %bitcast.23) | data formatting | bytes 294912
  7.6 0.0 copy-start
  7.6 0.6 copy-done
  8.2 1.0 %convolution_convert_fusion = bf16[16,12288]{1,0:T(8,128)(2,1)} fusion(bf16[6,12288]{1,0:T(8,128)(2,1)S(1)} %bitcast.20, s32[6]{0:T(128)S(1)} %bitcast.24), kind=kOutput, calls=%fused_computation | convolution fusion | flops 2556000 | bytes 540696 | tf_op jit(solution)/shard_map/dot_general | solution.py:30
  9.2 0.0 all-reduce.3.cloned.1.call-update
  9.2 0.0 copy-start.2
  9.3 0.6 copy-done.2
  9.9 0.6 dynamic-slice
  10.5 0.0 copy-start.1
  11.2 0.0 copy-done.1
  11.2 0.1 select_reduce_fusion
  11.3 38.3 %all-reduce.3.cloned.1.call-done = bf16[16,12288]{1,0:T(8,128)(2,1)} async-done(((bf16[16,12288]{1,0:T(8,128)(2,1)}), bf16[16,12288]{1,0:T(8,128)(2,1)}) %all-reduce.3.cloned.1.call-update) | async-done | bytes 393232
  49.5 1.0 %constant_dynamic-slice_fusion = bf16[4,12288]{1,0:T(4,128)(2,1)S(1)} fusion(bf16[16,12288]{1,0:T(8,128)(2,1)} %all-reduce.3.cloned.1.call-done, u32[]{:T(128)S(6)} %multiply.1), kind=kLoop, calls=%fused_computation.17 | loop fusion | bytes 196612
  50.5 0.7 %copy.10 = bf16[3,2,8,1024]{3,1,0,2:T(2,128)(2,1)} copy(bf16[3,2,8,1024]{3,2,1,0:T(8,128)(2,1)S(1)} %convert_element_type.25) | data formatting | bytes 196608 | tf_op jit(solution)/shard_map/convert_element_type | solution.py:33
  51.3 3.5 %all-to-all-start = ((bf16[3,2,8,1024]{3,1,0,2:T(2,128)(2,1)}), bf16[3,2,8,1024]{3,1,0,2:T(2,128)(2,1)S(1)}, u32[]{:S(2)}, u32[]{:S(2)}) async-start(bf16[3,2,8,1024]{3,1,0,2:T(2,128)(2,1)} %copy.10), calls=%async_computation | async-start | bytes 196608 | tf_op jit(solution)/shard_map/all_to_all | solution.py:38
  54.7 0.2 convert_reduce_fusion
  54.9 5.0 %all-to-all-done = bf16[3,2,8,1024]{3,1,0,2:T(2,128)(2,1)S(1)} async-done(((bf16[3,2,8,1024]{3,1,0,2:T(2,128)(2,1)}), bf16[3,2,8,1024]{3,1,0,2:T(2,128)(2,1)S(1)}, u32[]{:S(2)}, u32[]{:S(2)}) %all-to-all-start) | async-done | bytes 98336 | tf_op jit(solution)/shard_map/all_to_all | solution.py:38
  59.9 0.1 copy.11
  60.0 0.9 %convolution_bitcast_fusion = f32[3,16,1024]{2,1,0:T(8,128)} fusion(bf16[3,16,1024]{2,1,0:T(8,128)(2,1)S(1)} %squeeze.3, f32[16]{0:T(128)S(1)} %convert_reduce_fusion, s32[16]{0:T(128)S(1)} %broadcast_add_fusion), kind=kOutput, calls=%fused_computation.1 | convolution fusion | flops 1574656 | bytes 295040 | tf_op jit(solution)/shard_map/ij,cjm->cim/dot_general | solution.py:35
  (4 shorter events, 0.1 us)
Async XLA Ops:
  6.5 43.0 %all-reduce.3.cloned.1.call-start = ((), (), s32[]{:S(2)}) async-start(), calls=%async_computation.1 | async-start | bytes 786432
  7.6 0.7 copy-start
  9.2 0.7 copy-start.2
  10.5 0.7 copy-start.1
  51.3 8.7 %all-to-all-start = ((bf16[3,2,8,1024]{3,1,0,2:T(2,128)(2,1)}), bf16[3,2,8,1024]{3,1,0,2:T(2,128)(2,1)S(1)}, u32[]{:S(2)}, u32[]{:S(2)}) async-start(bf16[3,2,8,1024]{3,1,0,2:T(2,128)(2,1)} %copy.10), calls=%async_computation | async-start | bytes 196608 | tf_op jit(solution)/shard_map/all_to_all | solution.py:38
Sparse Core Ops, SparseCore 0:
  9.7 39.7 all-reduce.2
where the time goes:
time: 68.1 us; the launch traced here: 67.8 us
  waiting for transfers between devices  43.3 us (64%)
  between operations  14.1 us (21%)
  local copies, waits for them, and re-layouts  4.76 us (7%)
  starting transfers between devices  3.46 us (5%)
  matrix products  1.9 us (3%)
    unnamed x2, waiting for transfers between devices  38.3 us
    all_to_all x1, waiting for transfers between devices, shards(): lax.all_to_all(slab, 'blk', split_axis=2, concat_axis=1, tiled=True)  5.01 us
    unnamed x9, local copies, waits for them, and re-layouts  3.88 us
    all_to_all x1, starting transfers between devices, shards(): lax.all_to_all(slab, 'blk', split_axis=2, concat_axis=1, tiled=True)  3.46 us
  transfers between devices with their start and end apart: 2, of which 2 were waited for; matrix products, arithmetic and copies ran while one was open for 1% of the time, Pallas kernels for 0%

commit v1 on v0

v1 whole, which is shorter than its diff:
```python
import functools

import jax
import jax.numpy as jnp
from jax import lax
from jax.experimental import pallas as pl
from jax.experimental.pallas import tpu as pltpu
from jax.sharding import PartitionSpec as P

NT = 4
CAP = 2
LAYERS = 8
LANES = 128
TAG = 16
MESH = pl.DeviceIdType.MESH


def log2(n):
    assert n & (n - 1) == 0
    return n.bit_length() - 1


def spread_smoother(band, depth, slabs, cols, block):
    shape = (cols * depth, slabs * block)
    row = lax.broadcasted_iota(jnp.int32, shape, 0)
    col = lax.broadcasted_iota(jnp.int32, shape, 1)
    level = row & (depth - 1)
    within = col & (block - 1)
    levels = depth // slabs
    source = (col >> log2(block)) * levels + (within >> log2(cols))
    layer = level >> log2(depth // LAYERS)
    half = jnp.zeros(shape, jnp.int32)
    for n in range(LAYERS):
        half = jnp.where(layer == n, band[n], half)
    weight = jnp.maximum(half + 1 - jnp.abs(level - source), 0)
    weight = jnp.where(within < levels * cols, weight, 0).astype(jnp.float32)
    total = jnp.sum(weight, axis=1, keepdims=True) * (1.0 / cols)
    same = (row >> log2(depth)) == (within & (cols - 1))
    return jnp.where(same, weight / total, 0.0).astype(jnp.bfloat16)


def kernel(dims, tiles_hbm, region_hbm, band_hbm, out_ref, tiles, region, band, spread, pack, land, stage, grad,
           weights, in_sem, send1, recv1, send2, recv2):
    groups, slabs, count, levels, parts, cols, block = dims
    depth = levels * slabs
    per_tile = slabs // NT
    rows = levels * parts
    me, mine = lax.axis_index("ev"), lax.axis_index("blk")
    peers = [lax.rem(me + j, groups) for j in range(groups)]
    mates = [lax.rem(mine + j, slabs) for j in range(slabs)]

    barrier = pltpu.get_barrier_semaphore()
    for j in range(1, groups):
        pl.semaphore_signal(barrier, inc=1, device_id=(peers[j], mine), device_id_type=MESH)
    for j in range(1, slabs):
        pl.semaphore_signal(barrier, inc=1, device_id=(me, mates[j]), device_id_type=MESH)
    loads = [
        pltpu.make_async_copy(region_hbm, region, in_sem.at[0]),
        pltpu.make_async_copy(tiles_hbm, tiles, in_sem.at[1]),
        pltpu.make_async_copy(band_hbm, band, in_sem.at[2]),
    ]
    for load in loads:
        load.start()
    loads[0].wait()
    ids = [region[k] for k in range(count)]
    loads[1].wait()

    def pack_section(j):
        first, last = jnp.int32(-1), jnp.int32(-1)
        for k in range(count):
            here = (ids[k] >> log2(NT)) == peers[j]
            last = jnp.where(here, k, last)
            first = jnp.where(here & (first < 0), k, first)
        for slot, (entry, there) in enumerate(((first, first >= 0), (last, last != first))):
            entry = jnp.maximum(entry, 0)
            tile = jnp.where(there, region[entry] & (NT - 1), -1)
            pack[0, j, slot * 8 : slot * 8 + 8, :] = jnp.full((8, LANES), tile, jnp.int32).astype(jnp.bfloat16)
            values = tiles[entry].astype(jnp.float32)
            for k in range(parts):
                spread[j, slot, :, k, :] = values[:, k * LANES : (k + 1) * LANES]
            for c in range(3):
                piece = spread[j, slot, c * levels : (c + 1) * levels].reshape(rows, LANES)
                at = TAG + slot * rows
                pack[c, j, at : at + rows, :] = piece.astype(jnp.bfloat16)

    def send_section(c, j):
        at = pl.ds(0, TAG + CAP * rows) if c == 0 else pl.ds(TAG, CAP * rows)
        copy = pltpu.make_async_remote_copy(
            src_ref=pack.at[c, j, at],
            dst_ref=land.at[c, j, at],
            send_sem=send1.at[c, j],
            recv_sem=recv1.at[c, j],
            device_id=(peers[j], mine),
            device_id_type=MESH,
        )
        copy.start()
        return copy

    def send_columns(c, j):
        copy = pltpu.make_async_remote_copy(
            src_ref=stage.at[c, mates[j]],
            dst_ref=grad.at[c, mine],
            send_sem=send2.at[c, j],
            recv_sem=recv2.at[c, j],
            device_id=(me, mates[j]),
            device_id_type=MESH,
        )
        copy.start()
        return copy

    order = list(range(groups - 1, 0, -1))
    sections, columns = {}, {}
    for n, j in enumerate(order):
        pack_section(j)
        if n == 0:
            pl.semaphore_wait(barrier, groups + slabs - 2)
        sections[0, j] = send_section(0, j)
    for c in range(1, 3):
        for j in order:
            sections[c, j] = send_section(c, j)
    pack_section(0)
    loads[2].wait()
    weights[...] = spread_smoother(band, depth, slabs, cols, block)

    for c in range(3):
        sums = [jnp.zeros((levels * parts // 8, 8, LANES), jnp.float32) for _ in range(NT)]
        for j in range(groups):
            if j > 0:
                sections[c, j].wait_recv()
            held = pack if j == 0 else land
            tags = held[0, j, :TAG, :].astype(jnp.float32)
            for slot in range(CAP):
                at = TAG + slot * rows
                term = held[c, j, at : at + rows, :].astype(jnp.float32).reshape(rows // 8, 8, LANES)
                tag = tags[slot * 8 : slot * 8 + 8]
                for t in range(NT):
                    sums[t] += jnp.where((tag == t)[None], term, 0.0)
        for t in range(NT):
            total = sums[t].reshape(levels, parts, LANES)
            for q in range(per_tile):
                piece = total[:, q * cols : (q + 1) * cols, :].reshape(levels * cols, LANES)
                if block > levels * cols:
                    fill = jnp.zeros((block - levels * cols, LANES), jnp.float32)
                    piece = jnp.concatenate([piece, fill], axis=0)
                stage[c, t * per_tile + q] = piece.astype(jnp.bfloat16)
        for j in range(1, slabs):
            columns[c, j] = send_columns(c, j)
        grad[c, mine] = stage[c, mine]

    for c in range(3):
        for j in range(1, slabs):
            columns[c, j].wait_recv()
        gathered = grad[c].reshape(slabs * block, LANES)
        smooth = jnp.dot(weights[...], gathered, preferred_element_type=jnp.float32)
        for k in range(cols):
            out_ref[c, :, k * LANES : (k + 1) * LANES] = smooth[k * depth : (k + 1) * depth]
    for copy in list(sections.values()) + list(columns.values()):
        copy.wait_send()


def shards(kernel_tiles, region, band_width):
    tiles, ids = kernel_tiles[0, 0], region[0, 0]
    groups, slabs = lax.axis_size("ev"), lax.axis_size("blk")
    count, held, width = tiles.shape
    levels = held // 3
    depth = levels * slabs
    parts = width // LANES
    cols = NT * parts // slabs
    block = -(-levels * cols // 16) * 16
    dims = (groups, slabs, count, levels, parts, cols, block)
    rows = levels * parts
    message = TAG + CAP * rows
    return pl.pallas_call(
        functools.partial(kernel, dims),
        out_shape=jax.ShapeDtypeStruct((3, depth, cols * LANES), jnp.float32),
        in_specs=[pl.BlockSpec(memory_space=pl.ANY)] * 3,
        out_specs=pl.BlockSpec(memory_space=pltpu.VMEM),
        scratch_shapes=[
            pltpu.VMEM(tiles.shape, jnp.bfloat16),
            pltpu.SMEM(ids.shape, jnp.int32),
            pltpu.SMEM(band_width.shape, jnp.int32),
            pltpu.VMEM((groups, CAP, held, parts, LANES), jnp.float32),
            pltpu.VMEM((3, groups, message, LANES), jnp.bfloat16),
            pltpu.VMEM((3, groups, message, LANES), jnp.bfloat16),
            pltpu.VMEM((3, slabs, block, LANES), jnp.bfloat16),
            pltpu.VMEM((3, slabs, block, LANES), jnp.bfloat16),
            pltpu.VMEM((cols * depth, slabs * block), jnp.bfloat16),
            pltpu.SemaphoreType.DMA((3,)),
            pltpu.SemaphoreType.DMA((3, groups)),
            pltpu.SemaphoreType.DMA((3, groups)),
            pltpu.SemaphoreType.DMA((3, slabs)),
            pltpu.SemaphoreType.DMA((3, slabs)),
        ],
        compiler_params=pltpu.CompilerParams(
            collective_id=0, has_side_effects=True, vmem_limit_bytes=48 * 1024 * 1024
        ),
    )(tiles, ids, band_width)


def solution(mesh):
    in_specs = (P("ev", "blk", None, None, None), P("ev", "blk", None), P())
    out_specs = P(None, None, ("ev", "blk"))
    return jax.shard_map(shards, mesh=mesh, in_specs=in_specs, out_specs=out_specs, check_vma=False)
```

time: 68.1 us -> 17.9 us (0.26)
  waiting for transfers between devices: 43.3 us -> 0 us
  Pallas kernels: 0 us -> 15.5 us
  between operations: 14.1 us -> 0.01 us
  starting transfers between devices: 3.46 us -> 0 us
  local copies, waits for them, and re-layouts: 4.76 us -> 2.28 us
  matrix products: 1.9 us -> 0 us
    unnamed x2 -> x0, waiting for transfers between devices: 38.3 us -> none
    pallas_call x0 -> x1, Pallas kernels: none -> 15.5 us  [shards(): pl.pallas_call(functools.partial(kernel, dims), out_shape=jax.ShapeDtypeS...]
    all_to_all x1 -> x0, waiting for transfers between devices: 5.01 us -> none  [shards(): lax.all_to_all(slab, 'blk', split_axis=2, concat_axis=1, tiled=True)]
    all_to_all x1 -> x0, starting transfers between devices: 3.46 us -> none  [shards(): lax.all_to_all(slab, 'blk', split_axis=2, concat_axis=1, tiled=True)]
    dot_general x2 -> x0, matrix products: 1.9 us -> none  [the longest x1 1 us: shards(): jnp.dot(onehot, flat, preferred_element_type=jnp.float32)]
    unnamed x9 -> x7, local copies, waits for them, and re-layouts: 3.88 us -> 2.28 us
    convert_element_type x2 -> x0, local copies, waits for them, and re-layouts: 0.77 us -> none  [shards(): slab.reshape(3, depth_slab, slabs, NT * width // slabs).astype(jnp.bfloat16)]
  transfers between devices with their start and end apart: 2 -> 0, of which waited for: 2 -> 0; matrix products, arithmetic and copies ran while one was open for 1% -> 0% of each run, Pallas kernels for 0% -> 0%
where the time goes in v1:
time: 17.9 us; the launch traced here: 17.8 us
  Pallas kernels  15.5 us (87%)
  local copies, waits for them, and re-layouts  2.28 us (13%)
    pallas_call x1, Pallas kernels, shards(): pl.pallas_call(functools.partial(kernel, dims), out_shape=jax.ShapeDtypeS...  15.5 us
    unnamed x7, local copies, waits for them, and re-layouts  2.28 us

profile of v1, /device:TPU:0, one launch (start us, length us, event | category | flops | bytes accessed | tf_op | source)
XLA Modules:
  0.0 17.8 jit_solution(2555427586647752706)
XLA Ops:
  0.0 0.0 copy-start.1
  0.0 0.0 copy-start.2
  0.0 0.7 %copy-done.1 = s32[1,1,6]{2,1,0:T(1,128)S(1)} copy-done((s32[1,1,6]{2,1,0:T(1,128)S(1)}, s32[1,1,6]{2,1,0:T(1,128)}, u32[]{:S(2)}) %copy-start.1) | copy-done | bytes 48
  0.7 0.0 copy-done.2
  0.7 0.0 copy-start
  0.7 0.9 %copy-done = bf16[1,1,6,6,2048]{4,3,2,1,0:T(8,128)(2,1)S(1)} copy-done((bf16[1,1,6,6,2048]{4,3,2,1,0:T(8,128)(2,1)S(1)}, bf16[1,1,6,6,2048]{4,3,2,1,0:T(8,128)(2,1)}, u32[]{:S(2)}) %copy-start) | copy-done | bytes 147480
  1.6 15.5 %shard_map.37 = f32[3,16,1024]{2,1,0:T(8,128)S(1)} custom-call(bf16[6,6,2048]{2,1,0:T(8,128)(2,1)S(1)} %bitcast.2, s32[6]{0:T(128)S(1)} %bitcast.3, s32[8]{0:T(128)S(1)} %copy-done.2), custom_call_target="tpu_custom_call" | custom-call | tf_op jit(solution)/shard_map/pallas_call | solution.py:173
  17.1 0.7 %copy.5 = f32[3,16,1024]{2,1,0:T(8,128)} copy(f32[3,16,1024]{2,1,0:T(8,128)S(1)} %shard_map.37) | data formatting | bytes 393216
Async XLA Ops:
  0.0 0.7 %copy-start.1 = (s32[1,1,6]{2,1,0:T(1,128)S(1)}, s32[1,1,6]{2,1,0:T(1,128)}, u32[]{:S(2)}) copy-start(s32[1,1,6]{2,1,0:T(1,128)} %param.4) | copy-start | bytes 76
  0.0 0.7 %copy-start.2 = (s32[8]{0:T(128)S(1)}, s32[8]{0:T(128)}, u32[]{:S(2)}) copy-start(s32[8]{0:T(128)} %band_hbm.1) | copy-start | bytes 100
  0.7 0.9 %copy-start = (bf16[1,1,6,6,2048]{4,3,2,1,0:T(8,128)(2,1)S(1)}, bf16[1,1,6,6,2048]{4,3,2,1,0:T(8,128)(2,1)}, u32[]{:S(2)}) copy-start(bf16[1,1,6,6,2048]{4,3,2,1,0:T(8,128)(2,1)} %param.3) | copy-start | bytes 442372

commit v2 on v1

--- a/solution.py
+++ b/solution.py
@@ -42,18 +42,14 @@
 def kernel(dims, tiles_hbm, region_hbm, band_hbm, out_ref, tiles, region, band, spread, pack, land, stage, grad,
            weights, in_sem, send1, recv1, send2, recv2):
     groups, slabs, count, levels, parts, cols, block = dims
+    assert groups & (groups - 1) == 0 and slabs & (slabs - 1) == 0
     depth = levels * slabs
     per_tile = slabs // NT
     rows = levels * parts
     me, mine = lax.axis_index("ev"), lax.axis_index("blk")
-    peers = [lax.rem(me + j, groups) for j in range(groups)]
-    mates = [lax.rem(mine + j, slabs) for j in range(slabs)]
-
-    barrier = pltpu.get_barrier_semaphore()
-    for j in range(1, groups):
-        pl.semaphore_signal(barrier, inc=1, device_id=(peers[j], mine), device_id_type=MESH)
-    for j in range(1, slabs):
-        pl.semaphore_signal(barrier, inc=1, device_id=(me, mates[j]), device_id_type=MESH)
+    peers = [me ^ j for j in range(groups)]
+    mates = [mine ^ j for j in range(slabs)]
+
     loads = [
         pltpu.make_async_copy(region_hbm, region, in_sem.at[0]),
         pltpu.make_async_copy(tiles_hbm, tiles, in_sem.at[1]),
@@ -61,6 +57,11 @@
     ]
     for load in loads:
         load.start()
+    barrier = pltpu.get_barrier_semaphore()
+    for j in range(1, groups):
+        pl.semaphore_signal(barrier, inc=1, device_id=(peers[j], mine), device_id_type=MESH)
+    for j in range(1, slabs):
+        pl.semaphore_signal(barrier, inc=1, device_id=(me, mates[j]), device_id_type=MESH)
     loads[0].wait()
     ids = [region[k] for k in range(count)]
     loads[1].wait()
@@ -173,7 +174,7 @@
     return pl.pallas_call(
         functools.partial(kernel, dims),
         out_shape=jax.ShapeDtypeStruct((3, depth, cols * LANES), jnp.float32),
-        in_specs=[pl.BlockSpec(memory_space=pl.ANY)] * 3,
+        in_specs=[pl.BlockSpec(memory_space=pltpu.HBM)] * 3,
         out_specs=pl.BlockSpec(memory_space=pltpu.VMEM),
         scratch_shapes=[
             pltpu.VMEM(tiles.shape, jnp.bfloat16),
@@ -192,7 +193,7 @@
             pltpu.SemaphoreType.DMA((3, slabs)),
         ],
         compiler_params=pltpu.CompilerParams(
-            collective_id=0, has_side_effects=True, vmem_limit_bytes=48 * 1024 * 1024
+            collective_id=0, has_side_effects=True, vmem_limit_bytes=60 * 1024 * 1024
         ),
     )(tiles, ids, band_width)
 

time: 17.9 us -> 18 us (level)
  Pallas kernels: 15.5 us -> 16.2 us
  local copies, waits for them, and re-layouts: 2.28 us -> 1.62 us
    pallas_call x1, Pallas kernels: 15.5 us -> 16.2 us  [shards(): pl.pallas_call(functools.partial(kernel, dims), out_shape=jax.ShapeDtypeS...]
    unnamed x7 -> x1, local copies, waits for them, and re-layouts: 2.28 us -> 1.62 us
where the time goes in v2:
time: 18 us; the launch traced here: 17.9 us
  Pallas kernels  16.2 us (90%)
  local copies, waits for them, and re-layouts  1.62 us (9%)
    pallas_call x1, Pallas kernels, shards(): pl.pallas_call(functools.partial(kernel, dims), out_shape=jax.ShapeDtypeS...  16.2 us
    unnamed x1, local copies, waits for them, and re-layouts  1.62 us

profile of v2, /device:TPU:0, one launch (start us, length us, event | category | flops | bytes accessed | tf_op | source)
XLA Modules:
  0.0 17.9 jit_solution(9267361457355028713)
XLA Ops:
  0.0 16.2 %shard_map.37 = f32[3,16,1024]{2,1,0:T(8,128)} custom-call(bf16[6,6,2048]{2,1,0:T(8,128)(2,1)} %bitcast.2, s32[6]{0:T(128)} %bitcast.3, s32[8]{0:T(128)} %band_hbm.1), custom_call_target="tpu_custom_call" | custom-call | tf_op jit(solution)/shard_map/pallas_call | solution.py:174
  16.3 1.6 %copy.5 = f32[3,16,1024]{2,1,0:T(8,128)} copy(f32[3,16,1024]{2,1,0:T(8,128)} %shard_map.37) | data formatting | bytes 393216

commit v3 on v2

--- a/solution.py
+++ b/solution.py
@@ -173,7 +173,7 @@
     message = TAG + CAP * rows
     return pl.pallas_call(
         functools.partial(kernel, dims),
-        out_shape=jax.ShapeDtypeStruct((3, depth, cols * LANES), jnp.float32),
+        out_shape=pltpu.VMEM((3, depth, cols * LANES), jnp.float32),
         in_specs=[pl.BlockSpec(memory_space=pltpu.HBM)] * 3,
         out_specs=pl.BlockSpec(memory_space=pltpu.VMEM),
         scratch_shapes=[
@@ -193,9 +193,9 @@
             pltpu.SemaphoreType.DMA((3, slabs)),
         ],
         compiler_params=pltpu.CompilerParams(
-            collective_id=0, has_side_effects=True, vmem_limit_bytes=60 * 1024 * 1024
+            collective_id=0, has_side_effects=True, vmem_limit_bytes=48 * 1024 * 1024
         ),
-    )(tiles, ids, band_width)
+    )(*[pltpu.with_memory_space_constraint(a, pltpu.HBM) for a in (tiles, ids, band_width)])
 
 
 def solution(mesh):

time: 18 us -> 16.4 us (0.911)
  local copies, waits for them, and re-layouts: 1.62 us -> 0.68 us
  Pallas kernels: 16.2 us -> 15.6 us
    unnamed x1, local copies, waits for them, and re-layouts: 1.62 us -> 0.68 us
    pallas_call x1, Pallas kernels: 16.2 us -> 15.6 us  [shards(): pl.pallas_call(functools.partial(kernel, dims), out_shape=pltpu.VMEM((3,...]
where the time goes in v3:
time: 16.4 us; the launch traced here: 16.3 us
  Pallas kernels  15.6 us (95%)
  local copies, waits for them, and re-layouts  0.68 us (4%)
    pallas_call x1, Pallas kernels, shards(): pl.pallas_call(functools.partial(kernel, dims), out_shape=pltpu.VMEM((3,...  15.6 us
    unnamed x1, local copies, waits for them, and re-layouts  0.68 us

profile of v3, /device:TPU:0, one launch (start us, length us, event | category | flops | bytes accessed | tf_op | source)
XLA Modules:
  0.0 16.3 jit_solution(16318033340418481394)
XLA Ops:
  0.0 15.6 %shard_map.37 = f32[3,16,1024]{2,1,0:T(8,128)S(1)} custom-call(bf16[6,6,2048]{2,1,0:T(8,128)(2,1)} %bitcast.2, s32[6]{0:T(128)} %bitcast.3, s32[8]{0:T(128)} %band_hbm.1), custom_call_target="tpu_custom_call" | custom-call | tf_op jit(solution)/shard_map/pallas_call | solution.py:174
  15.6 0.7 %copy.5 = f32[3,16,1024]{2,1,0:T(8,128)} copy(f32[3,16,1024]{2,1,0:T(8,128)S(1)} %shard_map.37) | data formatting | bytes 393216

commit v4 on v3

--- a/solution.py
+++ b/solution.py
@@ -11,7 +11,6 @@
 CAP = 2
 LAYERS = 8
 LANES = 128
-TAG = 16
 MESH = pl.DeviceIdType.MESH
 
 
@@ -39,8 +38,8 @@
     return jnp.where(same, weight / total, 0.0).astype(jnp.bfloat16)
 
 
-def kernel(dims, tiles_hbm, region_hbm, band_hbm, out_ref, tiles, region, band, spread, pack, land, stage, grad,
-           weights, in_sem, send1, recv1, send2, recv2):
+def kernel(dims, tiles_hbm, region_hbm, band_hbm, out_ref, tiles, region, band, spread, tags, tags_in, pack, land,
+           stage, grad, weights, in_sem, send0, recv0, send1, recv1, send2, recv2):
     groups, slabs, count, levels, parts, cols, block = dims
     assert groups & (groups - 1) == 0 and slabs & (slabs - 1) == 0
     depth = levels * slabs
@@ -64,31 +63,45 @@
         pl.semaphore_signal(barrier, inc=1, device_id=(me, mates[j]), device_id_type=MESH)
     loads[0].wait()
     ids = [region[k] for k in range(count)]
-    loads[1].wait()
-
-    def pack_section(j):
+
+    def find(j):
         first, last = jnp.int32(-1), jnp.int32(-1)
         for k in range(count):
             here = (ids[k] >> log2(NT)) == peers[j]
             last = jnp.where(here, k, last)
             first = jnp.where(here & (first < 0), k, first)
-        for slot, (entry, there) in enumerate(((first, first >= 0), (last, last != first))):
-            entry = jnp.maximum(entry, 0)
-            tile = jnp.where(there, region[entry] & (NT - 1), -1)
-            pack[0, j, slot * 8 : slot * 8 + 8, :] = jnp.full((8, LANES), tile, jnp.int32).astype(jnp.bfloat16)
+        entries = [jnp.maximum(first, 0), jnp.maximum(last, 0)]
+        for slot, there in enumerate((first >= 0, last != first)):
+            tile = jnp.where(there, region[entries[slot]] & (NT - 1), -1)
+            tags[j, slot : slot + 1, :] = jnp.full((1, LANES), tile, jnp.int32)
+        return entries
+
+    def pack_section(j, entries):
+        for slot, entry in enumerate(entries):
             values = tiles[entry].astype(jnp.float32)
+            held = 3 * levels
             for k in range(parts):
-                spread[j, slot, :, k, :] = values[:, k * LANES : (k + 1) * LANES]
+                spread[j, slot, pl.ds(k, held, stride=parts), :] = values[:, k * LANES : (k + 1) * LANES]
             for c in range(3):
-                piece = spread[j, slot, c * levels : (c + 1) * levels].reshape(rows, LANES)
-                at = TAG + slot * rows
-                pack[c, j, at : at + rows, :] = piece.astype(jnp.bfloat16)
+                piece = spread[j, slot, c * rows : (c + 1) * rows, :]
+                pack[c, j, slot * rows : (slot + 1) * rows, :] = piece.astype(jnp.bfloat16)
+
+    def send_tags(j):
+        copy = pltpu.make_async_remote_copy(
+            src_ref=tags.at[j],
+            dst_ref=tags_in.at[j],
+            send_sem=send0.at[j],
+            recv_sem=recv0.at[j],
+            device_id=(peers[j], mine),
+            device_id_type=MESH,
+        )
+        copy.start()
+        return copy
 
     def send_section(c, j):
-        at = pl.ds(0, TAG + CAP * rows) if c == 0 else pl.ds(TAG, CAP * rows)
         copy = pltpu.make_async_remote_copy(
-            src_ref=pack.at[c, j, at],
-            dst_ref=land.at[c, j, at],
+            src_ref=pack.at[c, j],
+            dst_ref=land.at[c, j],
             send_sem=send1.at[c, j],
             recv_sem=recv1.at[c, j],
             device_id=(peers[j], mine),
@@ -110,30 +123,34 @@
         return copy
 
     order = list(range(groups - 1, 0, -1))
+    entries = [find(j) for j in range(groups)]
+    pl.semaphore_wait(barrier, groups + slabs - 2)
+    numbers = {j: send_tags(j) for j in order}
+    loads[1].wait()
     sections, columns = {}, {}
-    for n, j in enumerate(order):
-        pack_section(j)
-        if n == 0:
-            pl.semaphore_wait(barrier, groups + slabs - 2)
+    for j in order:
+        pack_section(j, entries[j])
         sections[0, j] = send_section(0, j)
     for c in range(1, 3):
         for j in order:
             sections[c, j] = send_section(c, j)
-    pack_section(0)
+    pack_section(0, entries[0])
     loads[2].wait()
     weights[...] = spread_smoother(band, depth, slabs, cols, block)
 
     for c in range(3):
-        sums = [jnp.zeros((levels * parts // 8, 8, LANES), jnp.float32) for _ in range(NT)]
+        sums = [jnp.zeros((rows // 8, 8, LANES), jnp.float32) for _ in range(NT)]
         for j in range(groups):
             if j > 0:
+                if c == 0:
+                    numbers[j].wait_recv()
                 sections[c, j].wait_recv()
             held = pack if j == 0 else land
-            tags = held[0, j, :TAG, :].astype(jnp.float32)
+            number = tags[j] if j == 0 else tags_in[j]
             for slot in range(CAP):
-                at = TAG + slot * rows
-                term = held[c, j, at : at + rows, :].astype(jnp.float32).reshape(rows // 8, 8, LANES)
-                tag = tags[slot * 8 : slot * 8 + 8]
+                term = held[c, j, slot * rows : (slot + 1) * rows, :].astype(jnp.float32)
+                term = term.reshape(rows // 8, 8, LANES)
+                tag = jnp.broadcast_to(number[slot : slot + 1], (8, LANES))
                 for t in range(NT):
                     sums[t] += jnp.where((tag == t)[None], term, 0.0)
         for t in range(NT):
@@ -155,7 +172,7 @@
         smooth = jnp.dot(weights[...], gathered, preferred_element_type=jnp.float32)
         for k in range(cols):
             out_ref[c, :, k * LANES : (k + 1) * LANES] = smooth[k * depth : (k + 1) * depth]
-    for copy in list(sections.values()) + list(columns.values()):
+    for copy in [*numbers.values(), *sections.values(), *columns.values()]:
         copy.wait_send()
 
 
@@ -170,7 +187,7 @@
     block = -(-levels * cols // 16) * 16
     dims = (groups, slabs, count, levels, parts, cols, block)
     rows = levels * parts
-    message = TAG + CAP * rows
+    message = CAP * rows
     return pl.pallas_call(
         functools.partial(kernel, dims),
         out_shape=pltpu.VMEM((3, depth, cols * LANES), jnp.float32),
@@ -180,13 +197,17 @@
             pltpu.VMEM(tiles.shape, jnp.bfloat16),
             pltpu.SMEM(ids.shape, jnp.int32),
             pltpu.SMEM(band_width.shape, jnp.int32),
-            pltpu.VMEM((groups, CAP, held, parts, LANES), jnp.float32),
+            pltpu.VMEM((groups, CAP, held * parts, LANES), jnp.float32),
+            pltpu.VMEM((groups, CAP, LANES), jnp.int32),
+            pltpu.VMEM((groups, CAP, LANES), jnp.int32),
             pltpu.VMEM((3, groups, message, LANES), jnp.bfloat16),
             pltpu.VMEM((3, groups, message, LANES), jnp.bfloat16),
             pltpu.VMEM((3, slabs, block, LANES), jnp.bfloat16),
             pltpu.VMEM((3, slabs, block, LANES), jnp.bfloat16),
             pltpu.VMEM((cols * depth, slabs * block), jnp.bfloat16),
             pltpu.SemaphoreType.DMA((3,)),
+            pltpu.SemaphoreType.DMA((groups,)),
+            pltpu.SemaphoreType.DMA((groups,)),
             pltpu.SemaphoreType.DMA((3, groups)),
             pltpu.SemaphoreType.DMA((3, groups)),
             pltpu.SemaphoreType.DMA((3, slabs)),

time: 16.4 us -> 16.2 us (0.988)
  Pallas kernels: 15.6 us -> 15.4 us
    pallas_call x1, Pallas kernels: 15.6 us -> 15.4 us  [shards(): pl.pallas_call(functools.partial(kernel, dims), out_shape=pltpu.VMEM((3,...]
where the time goes in v4:
time: 16.2 us; the launch traced here: 16.1 us
  Pallas kernels  15.4 us (95%)
  local copies, waits for them, and re-layouts  0.68 us (4%)
    pallas_call x1, Pallas kernels, shards(): pl.pallas_call(functools.partial(kernel, dims), out_shape=pltpu.VMEM((3,...  15.4 us
    unnamed x1, local copies, waits for them, and re-layouts  0.68 us

profile of v4, /device:TPU:0, one launch (start us, length us, event | category | flops | bytes accessed | tf_op | source)
XLA Modules:
  0.0 16.1 jit_solution(15931276535433010650)
XLA Ops:
  0.0 15.4 %shard_map.37 = f32[3,16,1024]{2,1,0:T(8,128)S(1)} custom-call(bf16[6,6,2048]{2,1,0:T(8,128)(2,1)} %bitcast.2, s32[6]{0:T(128)} %bitcast.3, s32[8]{0:T(128)} %band_hbm.1), custom_call_target="tpu_custom_call" | custom-call | tf_op jit(solution)/shard_map/pallas_call | solution.py:191
  15.4 0.7 %copy.5 = f32[3,16,1024]{2,1,0:T(8,128)} copy(f32[3,16,1024]{2,1,0:T(8,128)S(1)} %shard_map.37) | data formatting | bytes 393216

commit v5 on v4

--- a/solution.py
+++ b/solution.py
@@ -131,13 +131,16 @@
     for j in order:
         pack_section(j, entries[j])
         sections[0, j] = send_section(0, j)
-    for c in range(1, 3):
-        for j in order:
-            sections[c, j] = send_section(c, j)
     pack_section(0, entries[0])
     loads[2].wait()
     weights[...] = spread_smoother(band, depth, slabs, cols, block)
 
+    def send_next(c):
+        for j in order:
+            sections[c - 1, j].wait_send()
+            sections[c, j] = send_section(c, j)
+
+    send_next(1)
     for c in range(3):
         sums = [jnp.zeros((rows // 8, 8, LANES), jnp.float32) for _ in range(NT)]
         for j in range(groups):
@@ -164,6 +167,8 @@
         for j in range(1, slabs):
             columns[c, j] = send_columns(c, j)
         grad[c, mine] = stage[c, mine]
+        if c == 0:
+            send_next(2)
 
     for c in range(3):
         for j in range(1, slabs):
@@ -172,7 +177,7 @@
         smooth = jnp.dot(weights[...], gathered, preferred_element_type=jnp.float32)
         for k in range(cols):
             out_ref[c, :, k * LANES : (k + 1) * LANES] = smooth[k * depth : (k + 1) * depth]
-    for copy in [*numbers.values(), *sections.values(), *columns.values()]:
+    for copy in [*numbers.values(), *(sections[2, j] for j in order), *columns.values()]:
         copy.wait_send()
 
 

time: 16.2 us -> 18.7 us (1.15)
  Pallas kernels: 15.4 us -> 17.8 us
    pallas_call x1, Pallas kernels: 15.4 us -> 17.8 us  [shards(): pl.pallas_call(functools.partial(kernel, dims), out_shape=pltpu.VMEM((3,...]
where the time goes in v5:
time: 18.7 us; the launch traced here: 18.5 us
  Pallas kernels  17.8 us (95%)
  local copies, waits for them, and re-layouts  0.68 us (4%)
    pallas_call x1, Pallas kernels, shards(): pl.pallas_call(functools.partial(kernel, dims), out_shape=pltpu.VMEM((3,...  17.8 us
    unnamed x1, local copies, waits for them, and re-layouts  0.68 us

profile of v5, /device:TPU:0, one launch (start us, length us, event | category | flops | bytes accessed | tf_op | source)
XLA Modules:
  0.0 18.5 jit_solution(3757108622344306614)
XLA Ops:
  0.0 17.8 %shard_map.37 = f32[3,16,1024]{2,1,0:T(8,128)S(1)} custom-call(bf16[6,6,2048]{2,1,0:T(8,128)(2,1)} %bitcast.2, s32[6]{0:T(128)} %bitcast.3, s32[8]{0:T(128)} %band_hbm.1), custom_call_target="tpu_custom_call" | custom-call | tf_op jit(solution)/shard_map/pallas_call | solution.py:196
  17.8 0.7 %copy.5 = f32[3,16,1024]{2,1,0:T(8,128)} copy(f32[3,16,1024]{2,1,0:T(8,128)S(1)} %shard_map.37) | data formatting | bytes 393216

commit v6 on v4

--- a/solution.py
+++ b/solution.py
@@ -11,6 +11,7 @@
 CAP = 2
 LAYERS = 8
 LANES = 128
+CHUNKS = ((0, 3),)
 MESH = pl.DeviceIdType.MESH
 
 
@@ -84,7 +85,7 @@
                 spread[j, slot, pl.ds(k, held, stride=parts), :] = values[:, k * LANES : (k + 1) * LANES]
             for c in range(3):
                 piece = spread[j, slot, c * rows : (c + 1) * rows, :]
-                pack[c, j, slot * rows : (slot + 1) * rows, :] = piece.astype(jnp.bfloat16)
+                pack[j, c, slot * rows : (slot + 1) * rows, :] = piece.astype(jnp.bfloat16)
 
     def send_tags(j):
         copy = pltpu.make_async_remote_copy(
@@ -98,24 +99,24 @@
         copy.start()
         return copy
 
-    def send_section(c, j):
+    def send_section(n, j):
         copy = pltpu.make_async_remote_copy(
-            src_ref=pack.at[c, j],
-            dst_ref=land.at[c, j],
-            send_sem=send1.at[c, j],
-            recv_sem=recv1.at[c, j],
+            src_ref=pack.at[j, pl.ds(*CHUNKS[n])],
+            dst_ref=land.at[j, pl.ds(*CHUNKS[n])],
+            send_sem=send1.at[n, j],
+            recv_sem=recv1.at[n, j],
             device_id=(peers[j], mine),
             device_id_type=MESH,
         )
         copy.start()
         return copy
 
-    def send_columns(c, j):
+    def send_columns(n, j):
         copy = pltpu.make_async_remote_copy(
-            src_ref=stage.at[c, mates[j]],
-            dst_ref=grad.at[c, mine],
-            send_sem=send2.at[c, j],
-            recv_sem=recv2.at[c, j],
+            src_ref=stage.at[mates[j], pl.ds(*CHUNKS[n])],
+            dst_ref=grad.at[mine, pl.ds(*CHUNKS[n])],
+            send_sem=send2.at[n, j],
+            recv_sem=recv2.at[n, j],
             device_id=(me, mates[j]),
             device_id_type=MESH,
         )
@@ -131,24 +132,24 @@
     for j in order:
         pack_section(j, entries[j])
         sections[0, j] = send_section(0, j)
-    for c in range(1, 3):
+    for n in range(1, len(CHUNKS)):
         for j in order:
-            sections[c, j] = send_section(c, j)
+            sections[n, j] = send_section(n, j)
     pack_section(0, entries[0])
     loads[2].wait()
     weights[...] = spread_smoother(band, depth, slabs, cols, block)
 
-    for c in range(3):
+    def reduce(c, n, first):
         sums = [jnp.zeros((rows // 8, 8, LANES), jnp.float32) for _ in range(NT)]
         for j in range(groups):
-            if j > 0:
-                if c == 0:
+            if j > 0 and first:
+                if n == 0:
                     numbers[j].wait_recv()
-                sections[c, j].wait_recv()
+                sections[n, j].wait_recv()
             held = pack if j == 0 else land
             number = tags[j] if j == 0 else tags_in[j]
             for slot in range(CAP):
-                term = held[c, j, slot * rows : (slot + 1) * rows, :].astype(jnp.float32)
+                term = held[j, c, slot * rows : (slot + 1) * rows, :].astype(jnp.float32)
                 term = term.reshape(rows // 8, 8, LANES)
                 tag = jnp.broadcast_to(number[slot : slot + 1], (8, LANES))
                 for t in range(NT):
@@ -160,18 +161,23 @@
                 if block > levels * cols:
                     fill = jnp.zeros((block - levels * cols, LANES), jnp.float32)
                     piece = jnp.concatenate([piece, fill], axis=0)
-                stage[c, t * per_tile + q] = piece.astype(jnp.bfloat16)
+                stage[t * per_tile + q, c] = piece.astype(jnp.bfloat16)
+
+    for n, (low, size) in enumerate(CHUNKS):
+        for c in range(low, low + size):
+            reduce(c, n, c == low)
         for j in range(1, slabs):
-            columns[c, j] = send_columns(c, j)
-        grad[c, mine] = stage[c, mine]
-
-    for c in range(3):
+            columns[n, j] = send_columns(n, j)
+        grad[mine, pl.ds(low, size)] = stage[mine, pl.ds(low, size)]
+
+    for n, (low, size) in enumerate(CHUNKS):
         for j in range(1, slabs):
-            columns[c, j].wait_recv()
-        gathered = grad[c].reshape(slabs * block, LANES)
-        smooth = jnp.dot(weights[...], gathered, preferred_element_type=jnp.float32)
-        for k in range(cols):
-            out_ref[c, :, k * LANES : (k + 1) * LANES] = smooth[k * depth : (k + 1) * depth]
+            columns[n, j].wait_recv()
+        for c in range(low, low + size):
+            gathered = grad[:, c].reshape(slabs * block, LANES)
+            smooth = jnp.dot(weights[...], gathered, preferred_element_type=jnp.float32)
+            for k in range(cols):
+                out_ref[c, :, k * LANES : (k + 1) * LANES] = smooth[k * depth : (k + 1) * depth]
     for copy in [*numbers.values(), *sections.values(), *columns.values()]:
         copy.wait_send()
 
@@ -200,18 +206,18 @@
             pltpu.VMEM((groups, CAP, held * parts, LANES), jnp.float32),
             pltpu.VMEM((groups, CAP, LANES), jnp.int32),
             pltpu.VMEM((groups, CAP, LANES), jnp.int32),
-            pltpu.VMEM((3, groups, message, LANES), jnp.bfloat16),
-            pltpu.VMEM((3, groups, message, LANES), jnp.bfloat16),
-            pltpu.VMEM((3, slabs, block, LANES), jnp.bfloat16),
-            pltpu.VMEM((3, slabs, block, LANES), jnp.bfloat16),
+            pltpu.VMEM((groups, 3, message, LANES), jnp.bfloat16),
+            pltpu.VMEM((groups, 3, message, LANES), jnp.bfloat16),
+            pltpu.VMEM((slabs, 3, block, LANES), jnp.bfloat16),
+            pltpu.VMEM((slabs, 3, block, LANES), jnp.bfloat16),
             pltpu.VMEM((cols * depth, slabs * block), jnp.bfloat16),
             pltpu.SemaphoreType.DMA((3,)),
             pltpu.SemaphoreType.DMA((groups,)),
             pltpu.SemaphoreType.DMA((groups,)),
-            pltpu.SemaphoreType.DMA((3, groups)),
-            pltpu.SemaphoreType.DMA((3, groups)),
-            pltpu.SemaphoreType.DMA((3, slabs)),
-            pltpu.SemaphoreType.DMA((3, slabs)),
+            pltpu.SemaphoreType.DMA((len(CHUNKS), groups)),
+            pltpu.SemaphoreType.DMA((len(CHUNKS), groups)),
+            pltpu.SemaphoreType.DMA((len(CHUNKS), slabs)),
+            pltpu.SemaphoreType.DMA((len(CHUNKS), slabs)),
         ],
         compiler_params=pltpu.CompilerParams(
             collective_id=0, has_side_effects=True, vmem_limit_bytes=48 * 1024 * 1024

time: 16.2 us -> 16.2 us (level)
  no operation moved by 1% of the time
where the time goes in v6:
time: 16.2 us; the launch traced here: 16 us
  Pallas kernels  15.3 us (94%)
  local copies, waits for them, and re-layouts  0.68 us (4%)
    pallas_call x1, Pallas kernels, shards(): pl.pallas_call(functools.partial(kernel, dims), out_shape=pltpu.VMEM((3,...  15.3 us
    unnamed x1, local copies, waits for them, and re-layouts  0.68 us

profile of v6, /device:TPU:0, one launch (start us, length us, event | category | flops | bytes accessed | tf_op | source)
XLA Modules:
  0.0 16.0 jit_solution(1619859985460736805)
XLA Ops:
  0.0 15.3 %shard_map.37 = f32[3,16,1024]{2,1,0:T(8,128)S(1)} custom-call(bf16[6,6,2048]{2,1,0:T(8,128)(2,1)} %bitcast.2, s32[6]{0:T(128)} %bitcast.3, s32[8]{0:T(128)} %band_hbm.1), custom_call_target="tpu_custom_call" | custom-call | tf_op jit(solution)/shard_map/pallas_call | solution.py:197
  15.3 0.7 %copy.5 = f32[3,16,1024]{2,1,0:T(8,128)} copy(f32[3,16,1024]{2,1,0:T(8,128)S(1)} %shard_map.37) | data formatting | bytes 393216

commit v7 on v6

--- a/solution.py
+++ b/solution.py
@@ -125,49 +125,49 @@
 
     order = list(range(groups - 1, 0, -1))
     entries = [find(j) for j in range(groups)]
-    pl.semaphore_wait(barrier, groups + slabs - 2)
-    numbers = {j: send_tags(j) for j in order}
     loads[1].wait()
     sections, columns = {}, {}
-    for j in order:
+    for i, j in enumerate(order):
         pack_section(j, entries[j])
+        if i == 0:
+            pl.semaphore_wait(barrier, groups + slabs - 2)
         sections[0, j] = send_section(0, j)
     for n in range(1, len(CHUNKS)):
         for j in order:
             sections[n, j] = send_section(n, j)
+    numbers = {j: send_tags(j) for j in order}
     pack_section(0, entries[0])
     loads[2].wait()
     weights[...] = spread_smoother(band, depth, slabs, cols, block)
 
-    def reduce(c, n, first):
-        sums = [jnp.zeros((rows // 8, 8, LANES), jnp.float32) for _ in range(NT)]
+    def reduce(c, t):
+        total = jnp.zeros((rows // 8, 8, LANES), jnp.float32)
         for j in range(groups):
-            if j > 0 and first:
-                if n == 0:
-                    numbers[j].wait_recv()
-                sections[n, j].wait_recv()
             held = pack if j == 0 else land
             number = tags[j] if j == 0 else tags_in[j]
             for slot in range(CAP):
                 term = held[j, c, slot * rows : (slot + 1) * rows, :].astype(jnp.float32)
-                term = term.reshape(rows // 8, 8, LANES)
                 tag = jnp.broadcast_to(number[slot : slot + 1], (8, LANES))
-                for t in range(NT):
-                    sums[t] += jnp.where((tag == t)[None], term, 0.0)
-        for t in range(NT):
-            total = sums[t].reshape(levels, parts, LANES)
-            for q in range(per_tile):
-                piece = total[:, q * cols : (q + 1) * cols, :].reshape(levels * cols, LANES)
-                if block > levels * cols:
-                    fill = jnp.zeros((block - levels * cols, LANES), jnp.float32)
-                    piece = jnp.concatenate([piece, fill], axis=0)
-                stage[t * per_tile + q, c] = piece.astype(jnp.bfloat16)
+                total += jnp.where((tag == t)[None], term.reshape(rows // 8, 8, LANES), 0.0)
+        total = total.reshape(levels, parts, LANES)
+        for q in range(per_tile):
+            piece = total[:, q * cols : (q + 1) * cols, :].reshape(levels * cols, LANES)
+            if block > levels * cols:
+                fill = jnp.zeros((block - levels * cols, LANES), jnp.float32)
+                piece = jnp.concatenate([piece, fill], axis=0)
+            stage[t * per_tile + q, c] = piece.astype(jnp.bfloat16)
 
     for n, (low, size) in enumerate(CHUNKS):
-        for c in range(low, low + size):
-            reduce(c, n, c == low)
-        for j in range(1, slabs):
-            columns[n, j] = send_columns(n, j)
+        for j in order:
+            if n == 0:
+                numbers[j].wait_recv()
+            sections[n, j].wait_recv()
+        for other in range(NT - 1, -1, -1):
+            t = (mine >> log2(per_tile)) ^ other
+            for c in range(low, low + size):
+                reduce(c, t)
+            for j in range(max(other * per_tile, 1), (other + 1) * per_tile):
+                columns[n, j] = send_columns(n, j)
         grad[mine, pl.ds(low, size)] = stage[mine, pl.ds(low, size)]
 
     for n, (low, size) in enumerate(CHUNKS):

time: 16.2 us -> 15.8 us (0.975)
  Pallas kernels: 15.3 us -> 15 us
    pallas_call x1, Pallas kernels: 15.3 us -> 15 us  [shards(): pl.pallas_call(functools.partial(kernel, dims), out_shape=pltpu.VMEM((3,...]
where the time goes in v7:
time: 15.8 us; the launch traced here: 15.7 us
  Pallas kernels  15 us (95%)
  local copies, waits for them, and re-layouts  0.68 us (4%)
    pallas_call x1, Pallas kernels, shards(): pl.pallas_call(functools.partial(kernel, dims), out_shape=pltpu.VMEM((3,...  15 us
    unnamed x1, local copies, waits for them, and re-layouts  0.68 us

profile of v7, /device:TPU:0, one launch (start us, length us, event | category | flops | bytes accessed | tf_op | source)
XLA Modules:
  0.0 15.7 jit_solution(167227242894227264)
XLA Ops:
  0.0 15.0 %shard_map.37 = f32[3,16,1024]{2,1,0:T(8,128)S(1)} custom-call(bf16[6,6,2048]{2,1,0:T(8,128)(2,1)} %bitcast.2, s32[6]{0:T(128)} %bitcast.3, s32[8]{0:T(128)} %band_hbm.1), custom_call_target="tpu_custom_call" | custom-call | tf_op jit(solution)/shard_map/pallas_call | solution.py:197
  15.0 0.7 %copy.5 = f32[3,16,1024]{2,1,0:T(8,128)} copy(f32[3,16,1024]{2,1,0:T(8,128)S(1)} %shard_map.37) | data formatting | bytes 393216

commit v8 on v7

--- a/solution.py
+++ b/solution.py
@@ -11,7 +11,7 @@
 CAP = 2
 LAYERS = 8
 LANES = 128
-CHUNKS = ((0, 3),)
+CHUNKS = ((0, 2), (2, 1))
 MESH = pl.DeviceIdType.MESH
 
 

time: 15.8 us -> 16.3 us (1.032)
  Pallas kernels: 15 us -> 15.5 us
    pallas_call x1, Pallas kernels: 15 us -> 15.5 us  [shards(): pl.pallas_call(functools.partial(kernel, dims), out_shape=pltpu.VMEM((3,...]
where the time goes in v8:
time: 16.3 us; the launch traced here: 16.2 us
  Pallas kernels  15.5 us (95%)
  local copies, waits for them, and re-layouts  0.68 us (4%)
    pallas_call x1, Pallas kernels, shards(): pl.pallas_call(functools.partial(kernel, dims), out_shape=pltpu.VMEM((3,...  15.5 us
    unnamed x1, local copies, waits for them, and re-layouts  0.68 us

profile of v8, /device:TPU:0, one launch (start us, length us, event | category | flops | bytes accessed | tf_op | source)
XLA Modules:
  0.0 16.2 jit_solution(14365132580790818574)
XLA Ops:
  0.0 15.5 %shard_map.37 = f32[3,16,1024]{2,1,0:T(8,128)S(1)} custom-call(bf16[6,6,2048]{2,1,0:T(8,128)(2,1)} %bitcast.2, s32[6]{0:T(128)} %bitcast.3, s32[8]{0:T(128)} %band_hbm.1), custom_call_target="tpu_custom_call" | custom-call | tf_op jit(solution)/shard_map/pallas_call | solution.py:197
  15.5 0.7 %copy.5 = f32[3,16,1024]{2,1,0:T(8,128)} copy(f32[3,16,1024]{2,1,0:T(8,128)S(1)} %shard_map.37) | data formatting | bytes 393216

commit v9 on v7

--- a/solution.py
+++ b/solution.py
@@ -11,6 +11,7 @@
 CAP = 2
 LAYERS = 8
 LANES = 128
+LOADS = 3
 CHUNKS = ((0, 3),)
 MESH = pl.DeviceIdType.MESH
 
@@ -40,7 +41,7 @@
 
 
 def kernel(dims, tiles_hbm, region_hbm, band_hbm, out_ref, tiles, region, band, spread, tags, tags_in, pack, land,
-           stage, grad, weights, in_sem, send0, recv0, send1, recv1, send2, recv2):
+           partial, stage, grad, weights, in_sem, send0, recv0, send1, recv1, send2, recv2):
     groups, slabs, count, levels, parts, cols, block = dims
     assert groups & (groups - 1) == 0 and slabs & (slabs - 1) == 0
     depth = levels * slabs
@@ -52,9 +53,12 @@
 
     loads = [
         pltpu.make_async_copy(region_hbm, region, in_sem.at[0]),
-        pltpu.make_async_copy(tiles_hbm, tiles, in_sem.at[1]),
-        pltpu.make_async_copy(band_hbm, band, in_sem.at[2]),
+        pltpu.make_async_copy(band_hbm, band, in_sem.at[1]),
     ]
+    share = -(-count // LOADS)
+    for n, low in enumerate(range(0, count, share)):
+        part = pl.ds(low, min(share, count - low))
+        loads.append(pltpu.make_async_copy(tiles_hbm.at[part], tiles.at[part], in_sem.at[2 + n]))
     for load in loads:
         load.start()
     barrier = pltpu.get_barrier_semaphore()
@@ -124,8 +128,10 @@
         return copy
 
     order = list(range(groups - 1, 0, -1))
+    near, far = list(range(groups // 2)), list(range(groups // 2, groups))
     entries = [find(j) for j in range(groups)]
-    loads[1].wait()
+    for load in loads[2:]:
+        load.wait()
     sections, columns = {}, {}
     for i, j in enumerate(order):
         pack_section(j, entries[j])
@@ -137,18 +143,21 @@
             sections[n, j] = send_section(n, j)
     numbers = {j: send_tags(j) for j in order}
     pack_section(0, entries[0])
-    loads[2].wait()
+    loads[1].wait()
     weights[...] = spread_smoother(band, depth, slabs, cols, block)
 
-    def reduce(c, t):
-        total = jnp.zeros((rows // 8, 8, LANES), jnp.float32)
-        for j in range(groups):
+    def add_terms(total, c, t, sources):
+        for j in sources:
             held = pack if j == 0 else land
             number = tags[j] if j == 0 else tags_in[j]
             for slot in range(CAP):
                 term = held[j, c, slot * rows : (slot + 1) * rows, :].astype(jnp.float32)
                 tag = jnp.broadcast_to(number[slot : slot + 1], (8, LANES))
                 total += jnp.where((tag == t)[None], term.reshape(rows // 8, 8, LANES), 0.0)
+        return total
+
+    def reduce(c, t):
+        total = add_terms(partial[t, c].reshape(rows // 8, 8, LANES), c, t, far)
         total = total.reshape(levels, parts, LANES)
         for q in range(per_tile):
             piece = total[:, q * cols : (q + 1) * cols, :].reshape(levels * cols, LANES)
@@ -158,7 +167,15 @@
             stage[t * per_tile + q, c] = piece.astype(jnp.bfloat16)
 
     for n, (low, size) in enumerate(CHUNKS):
-        for j in order:
+        for j in near[1:]:
+            if n == 0:
+                numbers[j].wait_recv()
+            sections[n, j].wait_recv()
+        for c in range(low, low + size):
+            for t in range(NT):
+                zero = jnp.zeros((rows // 8, 8, LANES), jnp.float32)
+                partial[t, c] = add_terms(zero, c, t, near).reshape(rows, LANES)
+        for j in far:
             if n == 0:
                 numbers[j].wait_recv()
             sections[n, j].wait_recv()
@@ -208,10 +225,11 @@
             pltpu.VMEM((groups, CAP, LANES), jnp.int32),
             pltpu.VMEM((groups, 3, message, LANES), jnp.bfloat16),
             pltpu.VMEM((groups, 3, message, LANES), jnp.bfloat16),
+            pltpu.VMEM((NT, 3, rows, LANES), jnp.float32),
             pltpu.VMEM((slabs, 3, block, LANES), jnp.bfloat16),
             pltpu.VMEM((slabs, 3, block, LANES), jnp.bfloat16),
             pltpu.VMEM((cols * depth, slabs * block), jnp.bfloat16),
-            pltpu.SemaphoreType.DMA((3,)),
+            pltpu.SemaphoreType.DMA((2 + LOADS,)),
             pltpu.SemaphoreType.DMA((groups,)),
             pltpu.SemaphoreType.DMA((groups,)),
             pltpu.SemaphoreType.DMA((len(CHUNKS), groups)),

time: 15.8 us -> 15.9 us (level)
  no operation moved by 1% of the time
where the time goes in v9:
time: 15.9 us; the launch traced here: 15.7 us
  Pallas kernels  15 us (94%)
  local copies, waits for them, and re-layouts  0.68 us (4%)
    pallas_call x1, Pallas kernels, shards(): pl.pallas_call(functools.partial(kernel, dims), out_shape=pltpu.VMEM((3,...  15 us
    unnamed x1, local copies, waits for them, and re-layouts  0.68 us

profile of v9, /device:TPU:0, one launch (start us, length us, event | category | flops | bytes accessed | tf_op | source)
XLA Modules:
  0.0 15.7 jit_solution(14612320013557683009)
XLA Ops:
  0.0 15.0 %shard_map.37 = f32[3,16,1024]{2,1,0:T(8,128)S(1)} custom-call(bf16[6,6,2048]{2,1,0:T(8,128)(2,1)} %bitcast.2, s32[6]{0:T(128)} %bitcast.3, s32[8]{0:T(128)} %band_hbm.1), custom_call_target="tpu_custom_call" | custom-call | tf_op jit(solution)/shard_map/pallas_call | solution.py:214
  15.0 0.7 %copy.5 = f32[3,16,1024]{2,1,0:T(8,128)} copy(f32[3,16,1024]{2,1,0:T(8,128)S(1)} %shard_map.37) | data formatting | bytes 393216

commit v10 on v9

--- a/solution.py
+++ b/solution.py
@@ -105,8 +105,8 @@
 
     def send_section(n, j):
         copy = pltpu.make_async_remote_copy(
-            src_ref=pack.at[j, pl.ds(*CHUNKS[n])],
-            dst_ref=land.at[j, pl.ds(*CHUNKS[n])],
+            src_ref=pack.at[j, n],
+            dst_ref=land.at[j, n],
             send_sem=send1.at[n, j],
             recv_sem=recv1.at[n, j],
             device_id=(peers[j], mine),
@@ -137,10 +137,8 @@
         pack_section(j, entries[j])
         if i == 0:
             pl.semaphore_wait(barrier, groups + slabs - 2)
-        sections[0, j] = send_section(0, j)
-    for n in range(1, len(CHUNKS)):
-        for j in order:
-            sections[n, j] = send_section(n, j)
+        for c in range(3):
+            sections[c, j] = send_section(c, j)
     numbers = {j: send_tags(j) for j in order}
     pack_section(0, entries[0])
     loads[1].wait()
@@ -170,7 +168,8 @@
         for j in near[1:]:
             if n == 0:
                 numbers[j].wait_recv()
-            sections[n, j].wait_recv()
+            for c in range(low, low + size):
+                sections[c, j].wait_recv()
         for c in range(low, low + size):
             for t in range(NT):
                 zero = jnp.zeros((rows // 8, 8, LANES), jnp.float32)
@@ -178,7 +177,8 @@
         for j in far:
             if n == 0:
                 numbers[j].wait_recv()
-            sections[n, j].wait_recv()
+            for c in range(low, low + size):
+                sections[c, j].wait_recv()
         for other in range(NT - 1, -1, -1):
             t = (mine >> log2(per_tile)) ^ other
             for c in range(low, low + size):
@@ -232,8 +232,8 @@
             pltpu.SemaphoreType.DMA((2 + LOADS,)),
             pltpu.SemaphoreType.DMA((groups,)),
             pltpu.SemaphoreType.DMA((groups,)),
-            pltpu.SemaphoreType.DMA((len(CHUNKS), groups)),
-            pltpu.SemaphoreType.DMA((len(CHUNKS), groups)),
+            pltpu.SemaphoreType.DMA((3, groups)),
+            pltpu.SemaphoreType.DMA((3, groups)),
             pltpu.SemaphoreType.DMA((len(CHUNKS), slabs)),
             pltpu.SemaphoreType.DMA((len(CHUNKS), slabs)),
         ],

time: 15.9 us -> 16 us (level)
  Pallas kernels: 15 us -> 15.2 us
where the time goes in v10:
time: 16 us; the launch traced here: 15.9 us
  Pallas kernels  15.2 us (95%)
  local copies, waits for them, and re-layouts  0.68 us (4%)
    pallas_call x1, Pallas kernels, shards(): pl.pallas_call(functools.partial(kernel, dims), out_shape=pltpu.VMEM((3,...  15.2 us
    unnamed x1, local copies, waits for them, and re-layouts  0.68 us

profile of v10, /device:TPU:0, one launch (start us, length us, event | category | flops | bytes accessed | tf_op | source)
XLA Modules:
  0.0 15.9 jit_solution(15568700851567264887)
XLA Ops:
  0.0 15.2 %shard_map.37 = f32[3,16,1024]{2,1,0:T(8,128)S(1)} custom-call(bf16[6,6,2048]{2,1,0:T(8,128)(2,1)} %bitcast.2, s32[6]{0:T(128)} %bitcast.3, s32[8]{0:T(128)} %band_hbm.1), custom_call_target="tpu_custom_call" | custom-call | tf_op jit(solution)/shard_map/pallas_call | solution.py:214
  15.2 0.7 %copy.5 = f32[3,16,1024]{2,1,0:T(8,128)} copy(f32[3,16,1024]{2,1,0:T(8,128)S(1)} %shard_map.37) | data formatting | bytes 393216

commit v11 on v9

--- a/solution.py
+++ b/solution.py
@@ -59,13 +59,13 @@
     for n, low in enumerate(range(0, count, share)):
         part = pl.ds(low, min(share, count - low))
         loads.append(pltpu.make_async_copy(tiles_hbm.at[part], tiles.at[part], in_sem.at[2 + n]))
-    for load in loads:
-        load.start()
     barrier = pltpu.get_barrier_semaphore()
     for j in range(1, groups):
         pl.semaphore_signal(barrier, inc=1, device_id=(peers[j], mine), device_id_type=MESH)
     for j in range(1, slabs):
         pl.semaphore_signal(barrier, inc=1, device_id=(me, mates[j]), device_id_type=MESH)
+    for load in loads:
+        load.start()
     loads[0].wait()
     ids = [region[k] for k in range(count)]
 

time: 15.9 us -> 15.9 us (level)
  no operation moved by 1% of the time
where the time goes in v11:
time: 15.9 us; the launch traced here: 15.7 us
  Pallas kernels  15 us (94%)
  local copies, waits for them, and re-layouts  0.68 us (4%)
    pallas_call x1, Pallas kernels, shards(): pl.pallas_call(functools.partial(kernel, dims), out_shape=pltpu.VMEM((3,...  15 us
    unnamed x1, local copies, waits for them, and re-layouts  0.68 us

profile of v11, /device:TPU:0, one launch (start us, length us, event | category | flops | bytes accessed | tf_op | source)
XLA Modules:
  0.0 15.7 jit_solution(14419507941811585507)
XLA Ops:
  0.0 15.0 %shard_map.37 = f32[3,16,1024]{2,1,0:T(8,128)S(1)} custom-call(bf16[6,6,2048]{2,1,0:T(8,128)(2,1)} %bitcast.2, s32[6]{0:T(128)} %bitcast.3, s32[8]{0:T(128)} %band_hbm.1), custom_call_target="tpu_custom_call" | custom-call | tf_op jit(solution)/shard_map/pallas_call | solution.py:214
  15.0 0.7 %copy.5 = f32[3,16,1024]{2,1,0:T(8,128)} copy(f32[3,16,1024]{2,1,0:T(8,128)S(1)} %shard_map.37) | data formatting | bytes 393216
